TPU v7x, 32 devices: a whole 2x2x4 slice. The times are simulated.
32 devices in a mesh: groups: 2 (over x), loop: 16 (over z, y, core).
Axes of the slice: x: 2, y: 2, z: 4, core: 2. Of those that a mesh axis runs over, the one named last changes fastest.
Arguments:
- queries: bfloat16 [256, 4, 64, 128], P(('groups', 'loop')), parts along dimension 0, may hold values from -16 to 16
- new_keys: bfloat16 [256, 4, 4, 128], P(('groups', 'loop')), parts along dimension 0, may hold values from -8 to 8
- new_values: bfloat16 [256, 4, 4, 128], P(('groups', 'loop')), parts along dimension 0, may hold values from -12 to 12
- suffix_keys: bfloat16 [256, 256, 4, 128], P(('groups', 'loop')), parts along dimension 0, may hold values from -8 to 8
- suffix_values: bfloat16 [256, 256, 4, 128], P(('groups', 'loop')), parts along dimension 0, may hold values from -12 to 12
- suffix_len: int32 [256], P(('groups', 'loop')), parts along dimension 0, may hold values from 1 to 256, 16384 in all
- prefix_keys: bfloat16 [32, 64, 4, 128], P(('groups', 'loop')), parts along dimension 0, may hold values from -8 to 8
- prefix_values: bfloat16 [32, 64, 4, 128], P(('groups', 'loop')), parts along dimension 0, may hold values from -12 to 12
- block_ids: int32 [32], P(('groups', 'loop')), parts along dimension 0, may hold values from 0 to 15, each once
- block_lists: int32 [256, 4], P(('groups', 'loop')), parts along dimension 0, may hold values from 0 to 15, all different within a row
Outputs:
- attended: bfloat16 [256, 4, 64, 128], P(('groups', 'loop')), parts along dimension 0
There are 2 independent parts, one for each index of `groups`. A program takes and returns all parts, laid end to end along the dimension named above; each array names one. Nothing has to cross between parts.
Inputs may be any that keep to these rules, and one draw needn't show every extreme that they name: `block_ids`: each slot holds a different block. `block_lists`: each request names 4 different blocks; every block is named by some request. `suffix_len`: some request uses all 256 slots.
All inputs are finite; a program needn't handle non-finite values. No bound on the sum of `suffix_len` on one device may be relied on, other than what follows from the above.
Results may differ from a plain program's by a relative error of at most 0.004.
Values may be sent and summed in bfloat16 or wider, within the bound.
A program may use at most 64 MiB of HBM per device.

v0:
```python
import math

import jax
import jax.numpy as jnp
from jax import lax
from jax.sharding import PartitionSpec as P


def per_device(
    queries,
    new_keys,
    new_values,
    suffix_keys,
    suffix_values,
    suffix_len,
    prefix_keys,
    prefix_values,
    block_ids,
    block_lists,
):
    requests, decode_steps, head_count, head_width = queries.shape
    key_heads = new_keys.shape[2]
    group_size = head_count // key_heads
    score_scale = 1.0 / math.sqrt(head_width)
    per_request = decode_steps * group_size
    grouped = queries.reshape(requests, decode_steps, key_heads, group_size, head_width)
    grouped = grouped.transpose(0, 2, 1, 3, 4).reshape(requests, key_heads, per_request, head_width)
    suffix_scores = (
        jnp.einsum("rgmd,rkgd->rgmk", grouped, suffix_keys, preferred_element_type=jnp.float32)
        * score_scale
    )
    suffix_slots = suffix_keys.shape[1]
    suffix_shown = (jnp.arange(suffix_slots)[None, :] < suffix_len[:, None])[:, None, None, :]
    fresh_scores = (
        jnp.einsum("rgmd,rtgd->rgmt", grouped, new_keys, preferred_element_type=jnp.float32)
        * score_scale
    )
    step_of_row = jnp.arange(per_request) // group_size
    fresh_shown = (jnp.arange(decode_steps)[None, :] <= step_of_row[:, None])[None, None]
    local_top = jnp.maximum(
        jnp.max(jnp.where(suffix_shown, suffix_scores, -jnp.inf), axis=-1),
        jnp.max(jnp.where(fresh_shown, fresh_scores, -jnp.inf), axis=-1),
    )
    gathered = (
        lax.all_gather(prefix_keys, "loop", axis=0, tiled=True),
        lax.all_gather(prefix_values, "loop", axis=0, tiled=True),
        lax.all_gather(block_ids, "loop", axis=0, tiled=True),
    )
    all_keys, all_values, all_ids = gathered
    block_count = all_ids.shape[0]
    named_count = block_lists.shape[1]
    block_size = all_keys.shape[1]
    matches = all_ids[None, None, :] == block_lists[:, :, None]
    slots = jnp.sum(
        jnp.where(matches, jnp.arange(block_count, dtype=jnp.int32)[None, None, :], 0), axis=2
    )
    prior_keys = all_keys[slots].reshape(requests, named_count * block_size, key_heads, head_width)
    prior_values = all_values[slots].reshape(
        requests, named_count * block_size, key_heads, head_width
    )
    prior_scores = (
        jnp.einsum("rgmd,rkgd->rgmk", grouped, prior_keys, preferred_element_type=jnp.float32)
        * score_scale
    )
    whole_top = jnp.maximum(local_top, jnp.max(prior_scores, axis=-1))
    suffix_weights = jnp.where(suffix_shown, jnp.exp(suffix_scores - whole_top[..., None]), 0.0)
    fresh_weights = jnp.where(fresh_shown, jnp.exp(fresh_scores - whole_top[..., None]), 0.0)
    sums = jnp.sum(suffix_weights, axis=-1) + jnp.sum(fresh_weights, axis=-1)
    weighted = jnp.einsum(
        "rgmk,rkgd->rgmd",
        suffix_weights.astype(jnp.bfloat16),
        suffix_values,
        preferred_element_type=jnp.float32,
    )
    weighted = weighted + jnp.einsum(
        "rgmt,rtgd->rgmd",
        fresh_weights.astype(jnp.bfloat16),
        new_values,
        preferred_element_type=jnp.float32,
    )
    sums, weighted = (sums, weighted)
    prior_weights = jnp.exp(prior_scores - whole_top[..., None])
    sums = sums + jnp.sum(prior_weights, axis=-1)
    weighted = weighted + jnp.einsum(
        "rgmk,rkgd->rgmd",
        prior_weights.astype(jnp.bfloat16),
        prior_values,
        preferred_element_type=jnp.float32,
    )
    mixed = weighted / sums[..., None]
    mixed = mixed.reshape(requests, key_heads, decode_steps, group_size, head_width).transpose(
        0, 2, 1, 3, 4
    )
    return mixed.reshape(requests, decode_steps, head_count, head_width).astype(jnp.bfloat16)


def solution(mesh):
    in_specs = (
        P(("groups", "loop"), None, None, None),
        P(("groups", "loop"), None, None, None),
        P(("groups", "loop"), None, None, None),
        P(("groups", "loop"), None, None, None),
        P(("groups", "loop"), None, None, None),
        P(("groups", "loop")),
        P(("groups", "loop"), None, None, None),
        P(("groups", "loop"), None, None, None),
        P(("groups", "loop")),
        P(("groups", "loop"), None),
    )
    out_specs = P(("groups", "loop"), None, None, None)
    return jax.shard_map(
        per_device, mesh=mesh, in_specs=in_specs, out_specs=out_specs, check_vma=False
    )
```

profile of v0, /device:TPU:0, one launch (start us, length us, event | category | flops | bytes accessed | tf_op | source)
XLA Modules:
  0.0 106.6 jit_solution(6860243202798953930)
XLA Ops:
  6.5 1.6 %copy.70 = bf16[1,64,4,128]{3,1,2,0:T(8,128)(2,1)} copy(bf16[1,64,4,128]{3,2,1,0:T(4,128)(2,1)} %param.16) | data formatting | bytes 131072 | tf_op args[6]
  8.2 0.0 all-gather.3.cloned.1.call-update
  8.2 0.0 all-gather.5.cloned.1.call-start
  8.2 1.5 %copy.76 = bf16[1,64,4,128]{3,1,2,0:T(8,128)(2,1)} copy(bf16[1,64,4,128]{3,2,1,0:T(4,128)(2,1)} %param.17) | data formatting | bytes 131072 | tf_op args[7]
  9.7 0.0 all-gather.5.cloned.1.call-update
  10.4 1.3 %dynamic-slice = u32[1]{0:T(128)} dynamic-slice(u32[32]{0:T(128)} %constant.41, u32[]{:T(128)S(6)} %add.41), dynamic_slice_sizes={1} | dynamic-slice | bytes 12
  11.7 0.7 dynamic-update-slice
  12.4 1.1 %copy.67 = bf16[8,4,4,16,128]{4,3,2,1,0:T(8,128)(2,1)S(1)} copy(bf16[8,4,4,16,128]{4,3,1,2,0:T(8,128)(2,1)} %bitcast.41) | data formatting | bytes 1048576 | tf_op jit(solution)/shard_map/transpose | solution.py:27
  13.5 13.8 %all-reduce = s32[16]{0:T(128)S(1)} all-reduce(s32[16]{0:T(128)S(1)} %dynamic-update-slice), channel_id=1, replica_groups=mesh['groups'=2,'loop'=16] {'loop'}, use_global_device_ids=true, to_apply=%add | all-reduce | flops 16 | bytes 128
  27.2 0.9 select_reduce_fusion.2
  28.2 0.1 copy.71
  28.2 0.1 reshape.102
  28.3 0.7 iota_compare_fusion
  29.1 1.1 %select_reduce_fusion.1 = (f32[8,4,64]{2,1,0:T(4,128)S(1)}, f32[8,4,64,4]{2,3,1,0:T(4,128)S(1)}) fusion(pred[64,4]{0,1:T(4,128)(4,1)S(1)} %iota_compare_fusion.1, bf16[8,4,64,128]{3,2,1,0:T(8,128)(2,1)S(1)} %bitcast.37, bf16[8,4,4,128]{3,2,1,0:T(4,128)(2,1)} %param.11), kind=kOutput, calls=%fused_computation.31 | convolution fusion | flops 2119680 | bytes 598272 | tf_op jit(solution)/shard_map/rgmd,rtgd->rgmt/dot_general | solution.py:35
  30.2 2.2 %select_reduce_fusion = (f32[8,4,64]{2,1,0:T(4,128)S(1)}, f32[8,4,64,256]{3,2,1,0:T(8,128)}) fusion(pred[8,256]{1,0:T(8,128)(4,1)S(1)} %iota_compare_fusion, bf16[8,4,64,128]{3,2,1,0:T(8,128)(2,1)S(1)} %bitcast.38, bf16[8,256,4,128]{3,2,1,0:T(4,128)(2,1)S(1)} %copy-done), kind=kOutput, calls=%fused_computation.14 | convolution fusion | flops 135788544 | bytes 4728832 | tf_op jit(solution)/shard_map/rgmd,rkgd->rgmk/dot_general | solution.py:29
  32.5 17.7 %all-gather.3.cloned.1.call-done = bf16[16,64,4,128]{3,1,2,0:T(8,128)(2,1)} async-done(((bf16[1,64,4,128]{3,1,2,0:T(8,128)(2,1)}), bf16[16,64,4,128]{3,1,2,0:T(8,128)(2,1)}) %all-gather.3.cloned.1.call-update) | async-done | bytes 1048592 | tf_op jit(solution)/shard_map/all_gather | solution.py:45
  50.2 3.3 %gather_fusion = bf16[32,64,4,128]{3,1,2,0:T(8,128)(2,1)} fusion(bf16[16,64,4,128]{3,1,2,0:T(8,128)(2,1)} %all-gather.3.cloned.1.call-done, s32[1024]{0:T(1024)S(1)} %pad_clamp_fusion), kind=kCustom, calls=%fused_computation | custom fusion | bytes 4194432 | tf_op jit(solution)/shard_map/gather | solution.py:57
  53.5 1.8 %copy.72 = bf16[32,64,4,128]{3,1,0,2:T(8,128)(2,1)S(1)} copy(bf16[32,64,4,128]{3,1,2,0:T(8,128)(2,1)} %gather_fusion) | data formatting | bytes 4194304 | tf_op jit(solution)/shard_map/gather | solution.py:57
  55.3 0.0 copy-start.4
  55.3 2.2 %bitcast_reduce_fusion = (f32[8,4,64]{2,1,0:T(4,128)S(1)}, f32[8,4,256,64]{2,3,1,0:T(8,128)}) fusion(bf16[8,4,64,128]{3,2,1,0:T(8,128)(2,1)S(1)} %bitcast.39, bf16[8,256,4,128]{3,1,0,2:T(8,128)(2,1)S(1)} %bitcast.36), kind=kOutput, calls=%fused_computation.3 | convolution fusion | flops 135264256 | bytes 4726784 | tf_op jit(solution)/shard_map/rgmd,rkgd->rgmk/dot_general | solution.py:62
  57.5 0.1 fusion.33
  57.6 0.4 fusion.35
  57.9 31.3 %all-gather.5.cloned.1.call-done = bf16[16,64,4,128]{3,1,2,0:T(8,128)(2,1)} async-done(((bf16[1,64,4,128]{3,1,2,0:T(8,128)(2,1)}), bf16[16,64,4,128]{3,1,2,0:T(8,128)(2,1)}) %all-gather.5.cloned.1.call-update) | async-done | bytes 1048592 | tf_op jit(solution)/shard_map/all_gather | solution.py:46
  89.3 3.4 %gather_fusion.1 = bf16[32,64,4,128]{3,1,2,0:T(8,128)(2,1)} fusion(bf16[16,64,4,128]{3,1,2,0:T(8,128)(2,1)} %all-gather.5.cloned.1.call-done, s32[1024]{0:T(1024)S(1)} %pad_clamp_fusion), kind=kCustom, calls=%fused_computation.1 | custom fusion | bytes 4194432 | tf_op jit(solution)/shard_map/gather | solution.py:58
  92.6 1.9 %copy.77 = bf16[32,64,4,128]{3,1,0,2:T(8,128)(2,1)S(1)} copy(bf16[32,64,4,128]{3,1,2,0:T(8,128)(2,1)} %gather_fusion.1) | data formatting | bytes 4194304 | tf_op jit(solution)/shard_map/gather | solution.py:58
  94.6 0.3 copy-done.1
  94.8 0.6 copy-done.2
  95.5 1.6 %fusion.11 = (f32[8,4,64]{2,1,0:T(4,128)S(1)}, f32[8,4,64]{2,1,0:T(4,128)S(1)}) fusion(f32[8,4,64,256]{3,2,1,0:T(8,128)S(1)} %copy-done.1, f32[8,4,64]{2,1,0:T(4,128)S(1)} %bitcast.45, pred[8,256]{1,0:T(8,128)(4,1)S(1)} %iota_compare_fusion, f32[8,4,256,64]{2,3,1,0:T(8,128)S(1)} %copy-done.2), kind=kLoop, calls=%fused_computation.17 | loop fusion | flops 3665920 | bytes 4220928 | tf_op jit(solution)/shard_map/reduce_sum | solution.py:68
  97.1 0.0 copy-done.3
  97.1 0.9 fusion.13
  98.0 0.9 fusion.22
  98.9 0.9 copy.79
  (14 shorter events, 0.1 us)
Async XLA Ops:
  6.5 23.7 %copy-start = (bf16[8,256,4,128]{3,2,1,0:T(4,128)(2,1)S(1)}, bf16[8,256,4,128]{3,2,1,0:T(4,128)(2,1)}, u32[]{:S(2)}) copy-start(bf16[8,256,4,128]{3,2,1,0:T(4,128)(2,1)} %param.13) | copy-start | bytes 6291460
  6.5 43.7 %all-gather.3.cloned.1.call-start = ((), (), s32[]{:S(2)}) async-start(), calls=%async_computation | async-start | bytes 1114112 | tf_op jit(solution)/shard_map/all_gather | solution.py:45
  8.2 81.1 %all-gather.5.cloned.1.call-start = ((), (), s32[]{:S(2)}) async-start(), calls=%async_computation.1 | async-start | bytes 1114112 | tf_op jit(solution)/shard_map/all_gather | solution.py:46
  55.3 2.3 %copy-start.4 = (bf16[8,4,4,128]{3,2,1,0:T(4,128)(2,1)S(1)}, bf16[8,4,4,128]{3,2,1,0:T(4,128)(2,1)}, u32[]{:S(2)}) copy-start(bf16[8,4,4,128]{3,2,1,0:T(4,128)(2,1)} %param.12) | copy-start | bytes 98308
  92.6 2.2 %copy-start.1 = (f32[8,4,64,256]{3,2,1,0:T(8,128)S(1)}, f32[8,4,64,256]{3,2,1,0:T(8,128)}, u32[]{:S(2)}) copy-start(f32[8,4,64,256]{3,2,1,0:T(8,128)} %get-tuple-element.10) | copy-start | bytes 6291460
  92.6 2.9 %copy-start.2 = (f32[8,4,256,64]{2,3,1,0:T(8,128)S(1)}, f32[8,4,256,64]{2,3,1,0:T(8,128)}, u32[]{:S(2)}) copy-start(f32[8,4,256,64]{2,3,1,0:T(8,128)} %get-tuple-element.8) | copy-start | bytes 6291460
  95.5 1.6 %copy-start.3 = (bf16[8,256,4,128]{3,2,1,0:T(4,128)(2,1)S(1)}, bf16[8,256,4,128]{3,2,1,0:T(4,128)(2,1)}, u32[]{:S(2)}) copy-start(bf16[8,256,4,128]{3,2,1,0:T(4,128)(2,1)} %param.14) | copy-start | bytes 6291460
Sparse Core Ops, SparseCore 0:
  9.5 40.6 all-gather.2
  52.4 36.8 all-gather.4
where the time goes:
time: 107 us
  waiting for transfers between devices  49.1 us (46%)
  local copies, waits for them, and re-layouts  18.5 us (17%)
  between operations  14.2 us (13%)
  blocking collectives  13.8 us (13%)
  matrix products  7.73 us (7%)
  other arithmetic  3.32 us (3%)
    all_gather x1, waiting for transfers between devices, per_device(): lax.all_gather(prefix_values, 'loop', axis=0, tiled=True)  31.3 us
    all_gather x1, waiting for transfers between devices, per_device(): lax.all_gather(prefix_keys, 'loop', axis=0, tiled=True)  17.7 us
    unnamed x1, blocking collectives  13.8 us
    unnamed x15, local copies, waits for them, and re-layouts  6.01 us
    gather x2, local copies, waits for them, and re-layouts, per_device(): all_values[slots]  5.31 us
    gather x2, local copies, waits for them, and re-layouts, per_device(): all_keys[slots]  5.09 us
    dot_general x1, matrix products, per_device(): jnp.einsum('rgmd,rkgd->rgmk', grouped, suffix_keys, preferred_element_typ...  2.22 us
    dot_general x1, matrix products, per_device(): jnp.einsum('rgmd,rkgd->rgmk', grouped, prior_keys, preferred_element_type...  2.16 us
  transfers between devices with their start and end apart: 2, of which 2 were waited for; matrix products, arithmetic and copies ran while one was open for 16% of the time, Pallas kernels for 0%

commit v1 on v0

v1 whole, which is shorter than its diff:
```python
import functools
import math

import jax
import jax.numpy as jnp
from jax import lax
from jax.experimental import pallas as pl
from jax.experimental.pallas import tpu as pltpu
from jax.sharding import PartitionSpec as P

F32 = jnp.float32
BF16 = jnp.bfloat16
NT = (((1,), (1,)), ((), ()))


def fold_of(count):
    chips = count // 2
    inner = 1 << ((chips.bit_length() - 1) // 2)
    return chips // inner, inner


def attend_kernel(
    outer,
    inner,
    q_hbm,
    fk_ref,
    fv_ref,
    sk_hbm,
    sv_hbm,
    len_ref,
    pk_ref,
    pv_ref,
    id_ref,
    lists_ref,
    out_ref,
    q_ref,
    sk_ref,
    sv_ref,
    wide,
    kbuf,
    vbuf,
    ibuf,
    slot_v,
    slot_s,
    top,
    tot,
    acc,
    prob,
    load_sem,
    line_recv,
    core_recv,
    a_send,
    b_send,
    core_send,
):
    requests, steps, head_count, width = q_ref.shape

    key_heads = fk_ref.shape[0] // (requests * steps)
    block = pk_ref.shape[0] // key_heads
    group = head_count // key_heads
    rows = steps * group
    suffix = sk_ref.shape[1] // key_heads
    named = lists_ref.shape[0]
    factor = math.log2(math.e) / math.sqrt(width)
    bufs = (kbuf, ibuf, vbuf)

    me = lax.axis_index("loop")
    core = lax.rem(me, 2)
    chip = me // 2
    pa = chip // inner
    pb = lax.rem(chip, inner)

    def device(a, b, c):
        return {"loop": (a * inner + b) * 2 + c}

    loads = [pltpu.make_async_copy(q_hbm, q_ref, load_sem.at[0])]
    for r in range(requests):
        loads.append(pltpu.make_async_copy(sk_hbm.at[r], sk_ref.at[r], load_sem.at[1 + 2 * r]))
        loads.append(pltpu.make_async_copy(sv_hbm.at[r], sv_ref.at[r], load_sem.at[2 + 2 * r]))
    for copy in loads:
        copy.start()

    neighbours = [
        (pa > 0, (pa - 1, pb, core)),
        (pa < outer - 1, (pa + 1, pb, core)),
        (pb > 0, (pa, pb - 1, core)),
        (pb < inner - 1, (pa, pb + 1, core)),
    ]
    barrier = pltpu.get_barrier_semaphore()
    count = jnp.int32(1)
    pl.semaphore_signal(
        barrier, inc=1, device_id=device(pa, pb, 1 - core), device_id_type=pl.DeviceIdType.MESH
    )
    for there, where in neighbours:
        count = count + there.astype(jnp.int32)

        @pl.when(there)
        def _(where=where):
            pl.semaphore_signal(
                barrier, inc=1, device_id=device(*where), device_id_type=pl.DeviceIdType.MESH
            )

    def split_rows(value, area, per_head):
        size = per_head * key_heads
        wide[area, pl.ds(0, size), :] = value.astype(F32)
        return [
            wide[area, pl.ds(g, per_head, stride=key_heads), :].astype(BF16)
            for g in range(key_heads)
        ]

    mine = pa * inner + pb
    for area, (source, target) in enumerate(((pk_ref, kbuf), (pv_ref, vbuf))):
        parts = split_rows(source[...], area, block)
        for g in range(key_heads):
            target[core, mine, pl.ds(g * block, block), :] = parts[g]
    ibuf[core, mine] = jnp.full(ibuf.shape[2:], id_ref[0], jnp.int32)

    pl.semaphore_wait(barrier, count)

    pending = []

    def send(kind, a, b, sem, recv, condition, where):
        copy = pltpu.make_async_remote_copy(
            src_ref=bufs[kind].at[core, a * inner + b],
            dst_ref=bufs[kind].at[core, a * inner + b],
            send_sem=sem,
            recv_sem=recv,
            device_id=device(*where),
            device_id_type=pl.DeviceIdType.MESH,
        )

        @pl.when(condition)
        def _():
            copy.start()

        return condition, copy

    def send_a(kind, a, condition, up):
        where = (pa + 1, pb, core) if up else (pa - 1, pb, core)
        ok = condition & ((pa < outer - 1) if up else (pa > 0))
        slot = a * inner + pb
        pending.append(
            send(kind, a, pb, a_send.at[kind, int(up), a], line_recv.at[kind, slot], ok, where)
        )

    def send_b(kind, a, b, condition, up, keep=True):
        where = (pa, pb + 1, core) if up else (pa, pb - 1, core)
        ok = condition & ((pb < inner - 1) if up else (pb > 0))
        slot = a * inner + b
        entry = send(kind, a, b, b_send.at[kind, int(up), slot], line_recv.at[kind, slot], ok, where)
        if keep:
            pending.append(entry)
        return entry

    def send_core(kind, a, b, condition):
        send(
            kind, a, b, core_send.at[kind], core_recv.at[kind], condition, (pa, pb, 1 - core)
        )

    def arrived(kind, a, b, condition):
        slot = a * inner + b

        @pl.when(condition)
        def _():
            here = bufs[kind].at[core, slot]
            pltpu.make_async_copy(here, here, line_recv.at[kind, slot]).wait()

    always = pa >= 0

    def own(kinds):
        for kind in kinds:
            send_a(kind, pa, always, True)
            send_a(kind, pa, always, False)
            send_b(kind, pa, pb, always, True)
            send_b(kind, pa, pb, always, False)
        for kind in kinds:
            send_core(kind, pa, pb, always)

    def line_event(t, kinds):
        for up, condition, a in ((True, pa >= t, pa - t), (False, pa + t < outer, pa + t)):
            a = jnp.clip(a, 0, outer - 1)
            for kind in kinds:
                arrived(kind, a, pb, condition)
                send_a(kind, a, condition, up)
                send_b(kind, a, pb, condition, True)
                send_b(kind, a, pb, condition, False)
                send_core(kind, a, pb, condition)

    def cross_one(u, a, condition, kinds):
        for up, here, b in ((True, pb >= u, pb - u), (False, pb + u < inner, pb + u)):
            here = here & condition
            b = jnp.clip(b, 0, inner - 1)
            for kind in kinds:
                arrived(kind, a, b, here)
                send_b(kind, a, b, here, up, keep=False)
                send_core(kind, a, b, here)

    def cross_wait(u, a, condition, kinds):
        for up, here, b in ((True, pb >= u, pb - u), (False, pb + u < inner, pb + u)):
            ok = here & condition & ((pb < inner - 1) if up else (pb > 0))
            slot = a * inner + jnp.clip(b, 0, inner - 1)
            for kind in kinds:

                @pl.when(ok)
                def _(kind=kind, slot=slot, up=up):
                    piece = bufs[kind].at[core, slot]
                    pltpu.make_async_copy(piece, piece, b_send.at[kind, int(up), slot]).wait()

    def order(t):
        if t == 0:
            return [(always, pa)]
        return [
            (pa >= t, jnp.clip(pa - t, 0, outer - 1)),
            (pa + t < outer, jnp.clip(pa + t, 0, outer - 1)),
        ]

    def cross_event(u, t, kinds):
        for condition, a in order(t):
            cross_one(u, a, condition, kinds)

    def query_rows(r, g):
        return q_ref[r, :, pl.ds(g * group, group), :].reshape(rows, width)

    def fresh_unit():
        loads[0].wait()
        fresh = requests * steps
        keys = split_rows(fk_ref[...], 0, fresh)
        values = split_rows(fv_ref[...], 1, fresh)
        row = lax.broadcasted_iota(jnp.int32, (requests * rows, fresh), 0)
        col = lax.broadcasted_iota(jnp.int32, (requests * rows, fresh), 1)
        shown = (row // rows == col // steps) & (
            lax.rem(col, steps) <= lax.rem(row, rows) // group
        )
        for g in range(key_heads):
            q = q_ref[:, :, pl.ds(g * group, group), :].reshape(requests * rows, width)
            s = lax.dot_general(q, keys[g], NT, preferred_element_type=F32) * factor
            s = jnp.where(shown, s, -jnp.inf)
            m = jnp.max(s, axis=1, keepdims=True)
            p = jnp.exp2(s - m)
            l = jnp.sum(p, axis=1, keepdims=True)
            o = jnp.dot(p.astype(BF16), values[g], preferred_element_type=F32)
            shape = (requests, rows, width)
            top[:, g] = jnp.broadcast_to(m, (requests * rows, width)).reshape(shape)
            tot[:, g] = jnp.broadcast_to(l, (requests * rows, width)).reshape(shape)
            acc[:, g] = o.reshape(shape)

    def suffix_unit(r):
        loads[1 + 2 * r].wait()
        keys = split_rows(sk_ref[r], 0, suffix)
        loads[2 + 2 * r].wait()
        values = split_rows(sv_ref[r], 1, suffix)
        shown = lax.broadcasted_iota(jnp.int32, (rows, suffix), 1) < len_ref[r]
        for g in range(key_heads):
            s = lax.dot_general(query_rows(r, g), keys[g], NT, preferred_element_type=F32)
            s = jnp.where(shown, s * factor, -jnp.inf)
            before = top[r, g][:, :1]
            m = jnp.maximum(before, jnp.max(s, axis=1, keepdims=True))
            p = jnp.exp2(s - m)
            shrink = jnp.exp2(before - m)
            l = tot[r, g][:, :1] * shrink + jnp.sum(p, axis=1, keepdims=True)
            o = jnp.dot(p.astype(BF16), values[g], preferred_element_type=F32)
            top[r, g] = jnp.broadcast_to(m, (rows, width))
            tot[r, g] = jnp.broadcast_to(l, (rows, width))
            acc[r, g] = acc[r, g] * shrink + o

    K = (0, 1)
    V = (2,)
    events = [lambda: cross_event(1, 0, K)] if inner > 1 else []
    if inner > 1:
        events.append(lambda: cross_event(1, 0, V))
    for t in range(1, outer):
        events.append(lambda t=t: line_event(t, K))
        events.append(lambda t=t: line_event(t, V))
    if inner > 1:
        events = events[2:] + events[:2]
    units = [functools.partial(suffix_unit, r) for r in range(requests)]

    own(K)
    own(V)
    fresh_unit()
    units.pop(0)()
    while units or events:
        if units:
            units.pop(0)()
        if events:
            events.pop(0)()

    for t in range(1, outer):
        if inner > 1:
            cross_event(1, t, K)

    def far(u, kinds):
        for t in range(outer):
            cross_event(u, t, kinds)

    if inner > 2:
        pl.loop(2, inner)(lambda u: far(u, K))

    def whole_wait(kind, side, sem):
        half = bufs[kind].at[side]
        pltpu.make_async_copy(half, half, sem).wait()

    whole_wait(0, 1 - core, core_recv.at[0])
    whole_wait(1, 1 - core, core_recv.at[1])

    half = outer * inner
    ids = ibuf[:, :, 0, :].reshape(2 * half, width)[:, :requests]
    place = lax.broadcasted_iota(jnp.int32, ids.shape, 0)
    for j in range(named):
        match = ids == lists_ref[pl.ds(j, 1), :]
        slot_v[pl.ds(j, 1), pl.ds(0, requests)] = jnp.max(
            jnp.where(match, place, 0), axis=0, keepdims=True
        )
    to_scalar = pltpu.make_async_copy(slot_v, slot_s, load_sem.at[0])
    to_scalar.start()
    to_scalar.wait()

    def gathered(buf, r, g):
        parts = []
        for j in range(named):
            slot = slot_s[j, r]
            parts.append(buf[slot // half, lax.rem(slot, half), pl.ds(g * block, block), :])
        return jnp.concatenate(parts, axis=0)

    @pl.loop(0, requests)
    def _(r):
        for g in range(key_heads):
            s = lax.dot_general(
                query_rows(r, g), gathered(kbuf, r, g), NT, preferred_element_type=F32
            )
            s = s * factor
            before = top[r, g][:, :1]
            m = jnp.maximum(before, jnp.max(s, axis=1, keepdims=True))
            p = jnp.exp2(s - m)
            shrink = jnp.exp2(before - m)
            l = tot[r, g][:, :1] * shrink + jnp.sum(p, axis=1, keepdims=True)
            prob[r, g] = p.astype(BF16)
            tot[r, g] = jnp.broadcast_to(l, (rows, width))
            acc[r, g] = acc[r, g] * shrink

    for t in range(1, outer):
        if inner > 1:
            cross_event(1, t, V)
    if inner > 2:
        pl.loop(2, inner)(lambda u: far(u, V))
    whole_wait(2, 1 - core, core_recv.at[2])

    @pl.loop(0, requests)
    def _(r):
        for g in range(key_heads):
            o = acc[r, g] + jnp.dot(
                prob[r, g], gathered(vbuf, r, g), preferred_element_type=F32
            )
            o = (o / tot[r, g]).astype(BF16)
            out_ref[r, :, pl.ds(g * group, group), :] = o.reshape(steps, group, width)

    for condition, copy in pending:

        @pl.when(condition)
        def _(copy=copy):
            copy.wait_send()

    if inner > 1:
        def drain(u):
            for t in range(outer):
                for condition, a in order(t):
                    cross_wait(u, a, condition, (0, 1, 2))

        if inner > 2:
            pl.loop(1, inner)(drain)
    for kind in range(3):
        whole_wait(kind, core, core_send.at[kind])


def per_device(
    loop,
    queries,
    new_keys,
    new_values,
    suffix_keys,
    suffix_values,
    suffix_len,
    prefix_keys,
    prefix_values,
    block_ids,
    block_lists,
):
    outer, inner = fold_of(loop)
    requests, steps, head_count, width = queries.shape
    key_heads = new_keys.shape[2]
    suffix = suffix_keys.shape[1]
    block = prefix_keys.shape[1]
    named = block_lists.shape[1]
    rows = steps * head_count // key_heads
    half = outer * inner
    vmem = pl.BlockSpec(memory_space=pltpu.VMEM)
    smem = pl.BlockSpec(memory_space=pltpu.SMEM)
    anywhere = pl.BlockSpec(memory_space=pltpu.HBM)
    kernel = functools.partial(attend_kernel, outer, inner)
    return pl.pallas_call(
        kernel,
        out_shape=jax.ShapeDtypeStruct(queries.shape, queries.dtype),
        in_specs=[
            anywhere,
            vmem,
            vmem,
            anywhere,
            anywhere,
            smem,
            vmem,
            vmem,
            smem,
            vmem,
        ],
        out_specs=vmem,
        scratch_shapes=[
            pltpu.VMEM(queries.shape, BF16),
            pltpu.VMEM((requests, suffix * key_heads, width), BF16),
            pltpu.VMEM((requests, suffix * key_heads, width), BF16),
            pltpu.VMEM((2, max(suffix, block, requests * steps) * key_heads, width), F32),
            pltpu.VMEM((2, half, key_heads * block, width), BF16),
            pltpu.VMEM((2, half, key_heads * block, width), BF16),
            pltpu.VMEM((2, half, 8, width), jnp.int32),
            pltpu.VMEM((8, 128), jnp.int32),
            pltpu.SMEM((8, 128), jnp.int32),
            pltpu.VMEM((requests, key_heads, rows, width), F32),
            pltpu.VMEM((requests, key_heads, rows, width), F32),
            pltpu.VMEM((requests, key_heads, rows, width), F32),
            pltpu.VMEM((requests, key_heads, rows, named * block), BF16),
            pltpu.SemaphoreType.DMA((1 + 2 * requests,)),
            pltpu.SemaphoreType.DMA((3, half)),
            pltpu.SemaphoreType.DMA((3,)),
            pltpu.SemaphoreType.DMA((3, 2, outer)),
            pltpu.SemaphoreType.DMA((3, 2, half)),
            pltpu.SemaphoreType.DMA((3,)),
        ],
        compiler_params=pltpu.CompilerParams(
            collective_id=0, has_side_effects=True, vmem_limit_bytes=60 * 1024 * 1024
        ),
        name="attend",
    )(
        queries,
        new_keys.reshape(-1, width),
        new_values.reshape(-1, width),
        suffix_keys.reshape(requests, suffix * key_heads, width),
        suffix_values.reshape(requests, suffix * key_heads, width),
        suffix_len,
        prefix_keys.reshape(-1, width),
        prefix_values.reshape(-1, width),
        block_ids,
        block_lists.T,
    )


def solution(mesh):
    lead = ("groups", "loop")
    in_specs = (
        P(lead, None, None, None),
        P(lead, None, None, None),
        P(lead, None, None, None),
        P(lead, None, None, None),
        P(lead, None, None, None),
        P(lead),
        P(lead, None, None, None),
        P(lead, None, None, None),
        P(lead),
        P(lead, None),
    )
    return jax.shard_map(
        functools.partial(per_device, mesh.shape["loop"]),
        mesh=mesh,
        in_specs=in_specs,
        out_specs=P(lead, None, None, None),
        check_vma=False,
    )
```

time: 107 us -> 34.3 us (0.32)
  waiting for transfers between devices: 49.1 us -> 0 us
  Pallas kernels: 0 us -> 31.6 us
  local copies, waits for them, and re-layouts: 18.5 us -> 1.87 us
  blocking collectives: 13.8 us -> 0 us
  between operations: 14.2 us -> 0.66 us
  matrix products: 7.73 us -> 0 us
  other arithmetic: 3.32 us -> 0 us
    all_gather x2 -> x0, waiting for transfers between devices: 49.1 us -> none  [the longest x1 31.3 us: per_device(): lax.all_gather(prefix_values, 'loop', axis=0, tiled=True)]
    pallas_call x0 -> x1, Pallas kernels: none -> 31.6 us  [per_device(): pl.pallas_call(kernel, out_shape=jax.ShapeDtypeStruct(queries.shape, quer...]
    unnamed x1 -> x0, blocking collectives: 13.8 us -> none
    gather x4 -> x0, local copies, waits for them, and re-layouts: 10.4 us -> none  [the longest x2 5.31 us: per_device(): all_values[slots]]
    dot_general x6 -> x0, matrix products: 7.73 us -> none  [the longest x1 2.22 us: per_device(): jnp.einsum('rgmd,rkgd->rgmk', grouped, suffix_keys, preferred_element_typ...]
    unnamed x15 -> x1, local copies, waits for them, and re-layouts: 6.01 us -> 1.87 us
    reduce_sum x3 -> x0, other arithmetic: 2.55 us -> none  [the longest x2 1.66 us: per_device(): sums = jnp.sum(suffix_weights, axis=-1) + jnp.sum(fresh_weights, axis=-1)]
    transpose x1 -> x0, local copies, waits for them, and re-layouts: 1.09 us -> none  [per_device(): grouped.transpose(0, 2, 1, 3, 4)]
  transfers between devices with their start and end apart: 2 -> 0, of which waited for: 2 -> 0; matrix products, arithmetic and copies ran while one was open for 16% -> 0% of each run, Pallas kernels for 0% -> 0%
where the time goes in v1:
time: 34.3 us; the launch traced here: 34.1 us
  Pallas kernels  31.6 us (92%)
  local copies, waits for them, and re-layouts  1.87 us (5%)
  between operations  0.66 us (2%)
    pallas_call x1, Pallas kernels, per_device(): pl.pallas_call(kernel, out_shape=jax.ShapeDtypeStruct(queries.shape, quer...  31.6 us
    unnamed x1, local copies, waits for them, and re-layouts  1.87 us

profile of v1, /device:TPU:0, one launch (start us, length us, event | category | flops | bytes accessed | tf_op | source)
XLA Modules:
  0.0 34.1 jit_solution(4271766234904596868)
XLA Ops:
  0.7 31.6 %attend.1 = bf16[8,4,64,128]{3,2,1,0:T(8,128)(2,1)} custom-call(bf16[8,4,64,128]{3,2,1,0:T(8,128)(2,1)} %q_hbm.1, bf16[128,128]{1,0:T(8,128)(2,1)} %bitcast.11, bf16[128,128]{1,0:T(8,128)(2,1)} %bitcast.12, bf16[8,1024,128]{2,1,0:T(8,128)(2,1)} %bitcast.7, bf16[8,1024,128]{2,1,0:T(8,128)(2,1)} %bitcast.8, s32[8]{0:T(128)} %len_ref.1, ...), custom_call_target="tpu_custom_call" | custom-call | tf_op jit(solution)/shard_map/attend/pallas_call | solution.py:400
  32.2 1.9 %copy.13 = bf16[8,4,64,128]{3,2,1,0:T(8,128)(2,1)} copy(bf16[8,4,64,128]{3,2,1,0:T(8,128)(2,1)} %attend.1) | data formatting | bytes 1048576

commit v2 on v1

--- a/solution.py
+++ b/solution.py
@@ -23,16 +23,24 @@
     outer,
     inner,
     q_hbm,
+    fk_hbm,
+    fv_hbm,
+    sk_hbm,
+    sv_hbm,
+    len_hbm,
+    pk_hbm,
+    pv_hbm,
+    id_ref,
+    lists_hbm,
+    out_ref,
     fk_ref,
     fv_ref,
-    sk_hbm,
-    sv_hbm,
-    len_ref,
     pk_ref,
     pv_ref,
-    id_ref,
     lists_ref,
-    out_ref,
+    len_ref,
+    fresh_k,
+    fresh_v,
     q_ref,
     sk_ref,
     sv_ref,
@@ -47,6 +55,7 @@
     acc,
     prob,
     load_sem,
+    small_sem,
     line_recv,
     core_recv,
     a_send,
@@ -73,6 +82,17 @@
     def device(a, b, c):
         return {"loop": (a * inner + b) * 2 + c}
 
+    pairs = (
+        (fk_hbm, fk_ref),
+        (fv_hbm, fv_ref),
+        (pk_hbm, pk_ref),
+        (pv_hbm, pv_ref),
+        (lists_hbm, lists_ref),
+        (len_hbm, len_ref),
+    )
+    small = [pltpu.make_async_copy(a, b, small_sem.at[i]) for i, (a, b) in enumerate(pairs)]
+    for i in (2, 3, 0, 1, 5, 4):
+        small[i].start()
     loads = [pltpu.make_async_copy(q_hbm, q_ref, load_sem.at[0])]
     for r in range(requests):
         loads.append(pltpu.make_async_copy(sk_hbm.at[r], sk_ref.at[r], load_sem.at[1 + 2 * r]))
@@ -110,6 +130,7 @@
 
     mine = pa * inner + pb
     for area, (source, target) in enumerate(((pk_ref, kbuf), (pv_ref, vbuf))):
+        small[2 + area].wait()
         parts = split_rows(source[...], area, block)
         for g in range(key_heads):
             target[core, mine, pl.ds(g * block, block), :] = parts[g]
@@ -221,64 +242,63 @@
     def query_rows(r, g):
         return q_ref[r, :, pl.ds(g * group, group), :].reshape(rows, width)
 
+    def wide_max(parts):
+        best = functools.reduce(jnp.maximum, parts)
+        return jnp.broadcast_to(jnp.max(best, axis=1, keepdims=True), best.shape)
+
+    def columns(x):
+        return [x[:, i : i + width] for i in range(0, x.shape[1], width)]
+
     def fresh_unit():
-        loads[0].wait()
         fresh = requests * steps
+        small[0].wait()
+        small[1].wait()
         keys = split_rows(fk_ref[...], 0, fresh)
         values = split_rows(fv_ref[...], 1, fresh)
-        row = lax.broadcasted_iota(jnp.int32, (requests * rows, fresh), 0)
-        col = lax.broadcasted_iota(jnp.int32, (requests * rows, fresh), 1)
-        shown = (row // rows == col // steps) & (
-            lax.rem(col, steps) <= lax.rem(row, rows) // group
-        )
-        for g in range(key_heads):
-            q = q_ref[:, :, pl.ds(g * group, group), :].reshape(requests * rows, width)
-            s = lax.dot_general(q, keys[g], NT, preferred_element_type=F32) * factor
-            s = jnp.where(shown, s, -jnp.inf)
-            m = jnp.max(s, axis=1, keepdims=True)
-            p = jnp.exp2(s - m)
-            l = jnp.sum(p, axis=1, keepdims=True)
-            o = jnp.dot(p.astype(BF16), values[g], preferred_element_type=F32)
-            shape = (requests, rows, width)
-            top[:, g] = jnp.broadcast_to(m, (requests * rows, width)).reshape(shape)
-            tot[:, g] = jnp.broadcast_to(l, (requests * rows, width)).reshape(shape)
-            acc[:, g] = o.reshape(shape)
+        for part, held in ((keys, fresh_k), (values, fresh_v)):
+            held[...] = jnp.zeros_like(held)
+            for g in range(key_heads):
+                held[g, pl.ds(0, fresh), :] = part[g]
+        loads[0].wait()
+        small[5].wait()
 
     def suffix_unit(r):
         loads[1 + 2 * r].wait()
         keys = split_rows(sk_ref[r], 0, suffix)
         loads[2 + 2 * r].wait()
         values = split_rows(sv_ref[r], 1, suffix)
-        shown = lax.broadcasted_iota(jnp.int32, (rows, suffix), 1) < len_ref[r]
+        slot = lax.broadcasted_iota(jnp.int32, (8, suffix), 1)
+        hidden = jnp.where(slot < len_ref[r], 0.0, -jnp.inf)
+        hidden = jnp.concatenate([hidden] * (rows // 8), axis=0)
+        row = lax.broadcasted_iota(jnp.int32, (rows, fresh_k.shape[1]), 0)
+        col = lax.broadcasted_iota(jnp.int32, (rows, fresh_k.shape[1]), 1) - r * steps
+        own_hidden = jnp.where((col >= 0) & (col <= row // group), 0.0, -jnp.inf)
+        biases = columns(hidden) + columns(own_hidden)
         for g in range(key_heads):
-            s = lax.dot_general(query_rows(r, g), keys[g], NT, preferred_element_type=F32)
-            s = jnp.where(shown, s * factor, -jnp.inf)
-            before = top[r, g][:, :1]
-            m = jnp.maximum(before, jnp.max(s, axis=1, keepdims=True))
-            p = jnp.exp2(s - m)
-            shrink = jnp.exp2(before - m)
-            l = tot[r, g][:, :1] * shrink + jnp.sum(p, axis=1, keepdims=True)
-            o = jnp.dot(p.astype(BF16), values[g], preferred_element_type=F32)
-            top[r, g] = jnp.broadcast_to(m, (rows, width))
-            tot[r, g] = jnp.broadcast_to(l, (rows, width))
-            acc[r, g] = acc[r, g] * shrink + o
+            all_keys = jnp.concatenate([keys[g], fresh_k[g]], axis=0)
+            all_values = jnp.concatenate([values[g], fresh_v[g]], axis=0)
+            s = lax.dot_general(query_rows(r, g), all_keys, NT, preferred_element_type=F32)
+            s = [x * factor + bias for x, bias in zip(columns(s), biases)]
+            m = wide_max(s)
+            p = [jnp.exp2(x - m) for x in s]
+            top[r, g] = m
+            tot[r, g] = functools.reduce(jnp.add, p)
+            p = jnp.concatenate(p, axis=1).astype(BF16)
+            acc[r, g] = jnp.dot(p, all_values, preferred_element_type=F32)
 
     K = (0, 1)
     V = (2,)
-    events = [lambda: cross_event(1, 0, K)] if inner > 1 else []
-    if inner > 1:
-        events.append(lambda: cross_event(1, 0, V))
+    events = []
     for t in range(1, outer):
         events.append(lambda t=t: line_event(t, K))
         events.append(lambda t=t: line_event(t, V))
     if inner > 1:
-        events = events[2:] + events[:2]
+        events.append(lambda: (cross_event(1, 0, K), cross_event(1, 0, V)))
     units = [functools.partial(suffix_unit, r) for r in range(requests)]
 
     own(K)
     own(V)
     fresh_unit()
-    units.pop(0)()
     while units or events:
         if units:
             units.pop(0)()
@@ -306,6 +326,7 @@
     half = outer * inner
     ids = ibuf[:, :, 0, :].reshape(2 * half, width)[:, :requests]
     place = lax.broadcasted_iota(jnp.int32, ids.shape, 0)
+    small[4].wait()
     for j in range(named):
         match = ids == lists_ref[pl.ds(j, 1), :]
         slot_v[pl.ds(j, 1), pl.ds(0, requests)] = jnp.max(
@@ -322,36 +343,37 @@
             parts.append(buf[slot // half, lax.rem(slot, half), pl.ds(g * block, block), :])
         return jnp.concatenate(parts, axis=0)
 
-    @pl.loop(0, requests)
-    def _(r):
+    def prior_unit(r):
         for g in range(key_heads):
             s = lax.dot_general(
                 query_rows(r, g), gathered(kbuf, r, g), NT, preferred_element_type=F32
             )
-            s = s * factor
-            before = top[r, g][:, :1]
-            m = jnp.maximum(before, jnp.max(s, axis=1, keepdims=True))
-            p = jnp.exp2(s - m)
+            s = [x * factor for x in columns(s)]
+            before = top[r, g]
+            m = jnp.maximum(before, wide_max(s))
+            p = [jnp.exp2(x - m) for x in s]
             shrink = jnp.exp2(before - m)
-            l = tot[r, g][:, :1] * shrink + jnp.sum(p, axis=1, keepdims=True)
-            prob[r, g] = p.astype(BF16)
-            tot[r, g] = jnp.broadcast_to(l, (rows, width))
-            acc[r, g] = acc[r, g] * shrink
-
-    for t in range(1, outer):
-        if inner > 1:
-            cross_event(1, t, V)
+            l = functools.reduce(jnp.add, p, tot[r, g] * shrink)
+            l = 1.0 / jnp.broadcast_to(jnp.sum(l, axis=1, keepdims=True), l.shape)
+            prob[r, g] = jnp.concatenate(p, axis=1).astype(BF16)
+            tot[r, g] = l
+            acc[r, g] = acc[r, g] * (shrink * l)
+
+    late = [lambda t=t: cross_event(1, t, V) for t in range(1, outer)] if inner > 1 else []
+    for r in range(requests):
+        prior_unit(r)
+        if late and r % 2 == 1:
+            late.pop(0)()
+    while late:
+        late.pop(0)()
     if inner > 2:
         pl.loop(2, inner)(lambda u: far(u, V))
     whole_wait(2, 1 - core, core_recv.at[2])
 
-    @pl.loop(0, requests)
-    def _(r):
+    for r in range(requests):
         for g in range(key_heads):
-            o = acc[r, g] + jnp.dot(
-                prob[r, g], gathered(vbuf, r, g), preferred_element_type=F32
-            )
-            o = (o / tot[r, g]).astype(BF16)
+            o = jnp.dot(prob[r, g], gathered(vbuf, r, g), preferred_element_type=F32)
+            o = (acc[r, g] + o * tot[r, g]).astype(BF16)
             out_ref[r, :, pl.ds(g * group, group), :] = o.reshape(steps, group, width)
 
     for condition, copy in pending:
@@ -393,6 +415,7 @@
     named = block_lists.shape[1]
     rows = steps * head_count // key_heads
     half = outer * inner
+    padded = -(-requests * steps // width) * width
     vmem = pl.BlockSpec(memory_space=pltpu.VMEM)
     smem = pl.BlockSpec(memory_space=pltpu.SMEM)
     anywhere = pl.BlockSpec(memory_space=pltpu.HBM)
@@ -400,20 +423,17 @@
     return pl.pallas_call(
         kernel,
         out_shape=jax.ShapeDtypeStruct(queries.shape, queries.dtype),
-        in_specs=[
-            anywhere,
-            vmem,
-            vmem,
-            anywhere,
-            anywhere,
-            smem,
-            vmem,
-            vmem,
-            smem,
-            vmem,
-        ],
+        in_specs=[anywhere] * 8 + [smem, anywhere],
         out_specs=vmem,
         scratch_shapes=[
+            pltpu.VMEM((requests * steps * key_heads, width), BF16),
+            pltpu.VMEM((requests * steps * key_heads, width), BF16),
+            pltpu.VMEM((block * key_heads, width), BF16),
+            pltpu.VMEM((block * key_heads, width), BF16),
+            pltpu.VMEM((named, requests), jnp.int32),
+            pltpu.SMEM((requests,), jnp.int32),
+            pltpu.VMEM((key_heads, padded, width), BF16),
+            pltpu.VMEM((key_heads, padded, width), BF16),
             pltpu.VMEM(queries.shape, BF16),
             pltpu.VMEM((requests, suffix * key_heads, width), BF16),
             pltpu.VMEM((requests, suffix * key_heads, width), BF16),
@@ -428,6 +448,7 @@
             pltpu.VMEM((requests, key_heads, rows, width), F32),
             pltpu.VMEM((requests, key_heads, rows, named * block), BF16),
             pltpu.SemaphoreType.DMA((1 + 2 * requests,)),
+            pltpu.SemaphoreType.DMA((6,)),
             pltpu.SemaphoreType.DMA((3, half)),
             pltpu.SemaphoreType.DMA((3,)),
             pltpu.SemaphoreType.DMA((3, 2, outer)),

time: 34.3 us -> 29.4 us (0.86)
  Pallas kernels: 31.6 us -> 26.7 us
    pallas_call x1, Pallas kernels: 31.6 us -> 26.7 us  [per_device(): pl.pallas_call(kernel, out_shape=jax.ShapeDtypeStruct(queries.shape, quer...]
where the time goes in v2:
time: 29.4 us; the launch traced here: 29.2 us
  Pallas kernels  26.7 us (91%)
  local copies, waits for them, and re-layouts  1.87 us (6%)
  between operations  0.66 us (2%)
    pallas_call x1, Pallas kernels, per_device(): pl.pallas_call(kernel, out_shape=jax.ShapeDtypeStruct(queries.shape, quer...  26.7 us
    unnamed x1, local copies, waits for them, and re-layouts  1.87 us

profile of v2, /device:TPU:0, one launch (start us, length us, event | category | flops | bytes accessed | tf_op | source)
XLA Modules:
  0.0 29.2 jit_solution(4916666336732497406)
XLA Ops:
  0.7 26.7 %attend.1 = bf16[8,4,64,128]{3,2,1,0:T(8,128)(2,1)} custom-call(bf16[8,4,64,128]{3,2,1,0:T(8,128)(2,1)} %q_hbm.1, bf16[128,128]{1,0:T(8,128)(2,1)} %bitcast.11, bf16[128,128]{1,0:T(8,128)(2,1)} %bitcast.12, bf16[8,1024,128]{2,1,0:T(8,128)(2,1)} %bitcast.7, bf16[8,1024,128]{2,1,0:T(8,128)(2,1)} %bitcast.8, s32[8]{0:T(128)} %len_hbm.1, ...), custom_call_target="tpu_custom_call" | custom-call | tf_op jit(solution)/shard_map/attend/pallas_call | solution.py:423
  27.4 1.9 %copy.13 = bf16[8,4,64,128]{3,2,1,0:T(8,128)(2,1)} copy(bf16[8,4,64,128]{3,2,1,0:T(8,128)(2,1)} %attend.1) | data formatting | bytes 1048576

commit v3 on v2

--- a/solution.py
+++ b/solution.py
@@ -136,7 +136,6 @@
             target[core, mine, pl.ds(g * block, block), :] = parts[g]
     ibuf[core, mine] = jnp.full(ibuf.shape[2:], id_ref[0], jnp.int32)
 
-    pl.semaphore_wait(barrier, count)
 
     pending = []
 
@@ -288,25 +287,32 @@
 
     K = (0, 1)
     V = (2,)
-    events = []
+    crossing = inner > 1
+    lines, cross_keys = [], []
     for t in range(1, outer):
-        events.append(lambda t=t: line_event(t, K))
-        events.append(lambda t=t: line_event(t, V))
-    if inner > 1:
-        events.append(lambda: (cross_event(1, 0, K), cross_event(1, 0, V)))
-    units = [functools.partial(suffix_unit, r) for r in range(requests)]
-
+        lines.append(lambda t=t: line_event(t, K))
+        if t > 1:
+            lines.append(lambda t=t: line_event(t - 1, V))
+    early = []
+    if crossing:
+        early.append((3, lambda: cross_event(1, 0, K)))
+        early.append((7, lambda: cross_event(1, 1, K)))
+    for i, event in enumerate(lines):
+        early.append((2 + i + (i > 0), event))
+    early.sort(key=lambda entry: entry[0])
+
+    fresh_unit()
+    pl.semaphore_wait(barrier, count)
     own(K)
     own(V)
-    fresh_unit()
-    while units or events:
-        if units:
-            units.pop(0)()
-        if events:
-            events.pop(0)()
-
-    for t in range(1, outer):
-        if inner > 1:
+    for r in range(requests):
+        suffix_unit(r)
+        while early and early[0][0] <= r:
+            early.pop(0)[1]()
+    for _, event in early:
+        event()
+    if crossing:
+        for t in range(2, outer):
             cross_event(1, t, K)
 
     def far(u, kinds):
@@ -359,10 +365,13 @@
             tot[r, g] = l
             acc[r, g] = acc[r, g] * (shrink * l)
 
-    late = [lambda t=t: cross_event(1, t, V) for t in range(1, outer)] if inner > 1 else []
+    late = [lambda: line_event(outer - 1, V)]
+    if crossing:
+        late = [lambda: cross_event(1, 0, V)] + late
+        late += [lambda t=t: cross_event(1, t, V) for t in range(1, outer)]
     for r in range(requests):
         prior_unit(r)
-        if late and r % 2 == 1:
+        if late and r % 2 == 0 or len(late) > 3:
             late.pop(0)()
     while late:
         late.pop(0)()
@@ -422,7 +431,7 @@
     kernel = functools.partial(attend_kernel, outer, inner)
     return pl.pallas_call(
         kernel,
-        out_shape=jax.ShapeDtypeStruct(queries.shape, queries.dtype),
+        out_shape=pltpu.VMEM(queries.shape, queries.dtype),
         in_specs=[anywhere] * 8 + [smem, anywhere],
         out_specs=vmem,
         scratch_shapes=[

time: 29.4 us -> 28.3 us (0.963)
  local copies, waits for them, and re-layouts: 1.87 us -> 0.8 us
    unnamed x1, local copies, waits for them, and re-layouts: 1.87 us -> 0.8 us
where the time goes in v3:
time: 28.3 us; the launch traced here: 28.1 us
  Pallas kernels  26.7 us (94%)
  local copies, waits for them, and re-layouts  0.8 us (3%)
  between operations  0.66 us (2%)
    pallas_call x1, Pallas kernels, per_device(): pl.pallas_call(kernel, out_shape=pltpu.VMEM(queries.shape, queries.dtype)...  26.7 us
    unnamed x1, local copies, waits for them, and re-layouts  0.8 us

profile of v3, /device:TPU:0, one launch (start us, length us, event | category | flops | bytes accessed | tf_op | source)
XLA Modules:
  0.0 28.1 jit_solution(16147296111958537070)
XLA Ops:
  0.7 26.7 %attend.1 = bf16[8,4,64,128]{3,2,1,0:T(8,128)(2,1)S(1)} custom-call(bf16[8,4,64,128]{3,2,1,0:T(8,128)(2,1)} %q_hbm.1, bf16[128,128]{1,0:T(8,128)(2,1)} %bitcast.11, bf16[128,128]{1,0:T(8,128)(2,1)} %bitcast.12, bf16[8,1024,128]{2,1,0:T(8,128)(2,1)} %bitcast.7, bf16[8,1024,128]{2,1,0:T(8,128)(2,1)} %bitcast.8, s32[8]{0:T(128)} %len_hbm.1, ...), custom_call_target="tpu_custom_call" | custom-call | tf_op jit(solution)/shard_map/attend/pallas_call | solution.py:432
  27.3 0.8 %copy.12 = bf16[8,4,64,128]{3,2,1,0:T(8,128)(2,1)} copy(bf16[8,4,64,128]{3,2,1,0:T(8,128)(2,1)S(1)} %attend.1) | data formatting | bytes 1048576

commit v4 on v3

--- a/solution.py
+++ b/solution.py
@@ -100,9 +100,11 @@
     for copy in loads:
         copy.start()
 
-    neighbours = [
-        (pa > 0, (pa - 1, pb, core)),
-        (pa < outer - 1, (pa + 1, pb, core)),
+    direct = outer <= 4
+    reach = outer if direct else 2
+    neighbours = [(pa >= d, (pa - d, pb, core)) for d in range(1, reach)]
+    neighbours += [(pa + d < outer, (pa + d, pb, core)) for d in range(1, reach)]
+    neighbours += [
         (pb > 0, (pa, pb - 1, core)),
         (pb < inner - 1, (pa, pb + 1, core)),
     ]
@@ -120,18 +122,19 @@
                 barrier, inc=1, device_id=device(*where), device_id_type=pl.DeviceIdType.MESH
             )
 
-    def split_rows(value, area, per_head):
+    def split_rows(source, area, per_head, heads=None):
         size = per_head * key_heads
-        wide[area, pl.ds(0, size), :] = value.astype(F32)
+        if heads is None or heads[0] == 0:
+            wide[area, pl.ds(0, size), :] = source[...].astype(F32)
         return [
             wide[area, pl.ds(g, per_head, stride=key_heads), :].astype(BF16)
-            for g in range(key_heads)
+            for g in (heads or range(key_heads))
         ]
 
     mine = pa * inner + pb
     for area, (source, target) in enumerate(((pk_ref, kbuf), (pv_ref, vbuf))):
         small[2 + area].wait()
-        parts = split_rows(source[...], area, block)
+        parts = split_rows(source, area, block)
         for g in range(key_heads):
             target[core, mine, pl.ds(g * block, block), :] = parts[g]
     ibuf[core, mine] = jnp.full(ibuf.shape[2:], id_ref[0], jnp.int32)
@@ -160,7 +163,7 @@
         ok = condition & ((pa < outer - 1) if up else (pa > 0))
         slot = a * inner + pb
         pending.append(
-            send(kind, a, pb, a_send.at[kind, int(up), a], line_recv.at[kind, slot], ok, where)
+            send(kind, a, pb, a_send.at[kind, int(up) + 1, a], line_recv.at[kind, slot], ok, where)
         )
 
     def send_b(kind, a, b, condition, up, keep=True):
@@ -189,8 +192,20 @@
 
     def own(kinds):
         for kind in kinds:
-            send_a(kind, pa, always, True)
-            send_a(kind, pa, always, False)
+            for d in range(1, reach):
+                for ok, a in ((pa + d < outer, pa + d), (pa >= d, pa - d)):
+                    slot = jnp.clip(a, 0, outer - 1)
+                    pending.append(
+                        send(
+                            kind,
+                            pa,
+                            pb,
+                            a_send.at[kind, 0, slot],
+                            line_recv.at[kind, mine],
+                            ok,
+                            (a, pb, core),
+                        )
+                    )
             send_b(kind, pa, pb, always, True)
             send_b(kind, pa, pb, always, False)
         for kind in kinds:
@@ -201,7 +216,8 @@
             a = jnp.clip(a, 0, outer - 1)
             for kind in kinds:
                 arrived(kind, a, pb, condition)
-                send_a(kind, a, condition, up)
+                if not direct:
+                    send_a(kind, a, condition, up)
                 send_b(kind, a, pb, condition, True)
                 send_b(kind, a, pb, condition, False)
                 send_core(kind, a, pb, condition)
@@ -252,8 +268,8 @@
         fresh = requests * steps
         small[0].wait()
         small[1].wait()
-        keys = split_rows(fk_ref[...], 0, fresh)
-        values = split_rows(fv_ref[...], 1, fresh)
+        keys = split_rows(fk_ref, 0, fresh)
+        values = split_rows(fv_ref, 1, fresh)
         for part, held in ((keys, fresh_k), (values, fresh_v)):
             held[...] = jnp.zeros_like(held)
             for g in range(key_heads):
@@ -261,11 +277,11 @@
         loads[0].wait()
         small[5].wait()
 
-    def suffix_unit(r):
-        loads[1 + 2 * r].wait()
-        keys = split_rows(sk_ref[r], 0, suffix)
-        loads[2 + 2 * r].wait()
-        values = split_rows(sv_ref[r], 1, suffix)
+    def suffix_unit(r, heads):
+        loads[1 + 2 * r].wait() if heads[0] == 0 else None
+        keys = split_rows(sk_ref.at[r], 0, suffix, heads)
+        loads[2 + 2 * r].wait() if heads[0] == 0 else None
+        values = split_rows(sv_ref.at[r], 1, suffix, heads)
         slot = lax.broadcasted_iota(jnp.int32, (8, suffix), 1)
         hidden = jnp.where(slot < len_ref[r], 0.0, -jnp.inf)
         hidden = jnp.concatenate([hidden] * (rows // 8), axis=0)
@@ -273,47 +289,58 @@
         col = lax.broadcasted_iota(jnp.int32, (rows, fresh_k.shape[1]), 1) - r * steps
         own_hidden = jnp.where((col >= 0) & (col <= row // group), 0.0, -jnp.inf)
         biases = columns(hidden) + columns(own_hidden)
-        for g in range(key_heads):
-            all_keys = jnp.concatenate([keys[g], fresh_k[g]], axis=0)
-            all_values = jnp.concatenate([values[g], fresh_v[g]], axis=0)
-            s = lax.dot_general(query_rows(r, g), all_keys, NT, preferred_element_type=F32)
-            s = [x * factor + bias for x, bias in zip(columns(s), biases)]
-            m = wide_max(s)
-            p = [jnp.exp2(x - m) for x in s]
-            top[r, g] = m
-            tot[r, g] = functools.reduce(jnp.add, p)
-            p = jnp.concatenate(p, axis=1).astype(BF16)
-            acc[r, g] = jnp.dot(p, all_values, preferred_element_type=F32)
+        held = [(fresh_k[g], fresh_v[g]) for g in heads]
+        s = [
+            lax.dot_general(
+                query_rows(r, g),
+                jnp.concatenate([k, more[0]], axis=0),
+                NT,
+                preferred_element_type=F32,
+            )
+            for g, k, more in zip(heads, keys, held)
+        ]
+        s = [[x * factor + bias for x, bias in zip(columns(x), biases)] for x in s]
+        m = [wide_max(x) for x in s]
+        p = [[jnp.exp2(x - most) for x in part] for part, most in zip(s, m)]
+        o = [
+            jnp.dot(
+                jnp.concatenate(part, axis=1).astype(BF16),
+                jnp.concatenate([v, more[1]], axis=0),
+                preferred_element_type=F32,
+            )
+            for part, v, more in zip(p, values, held)
+        ]
+        for i, g in enumerate(heads):
+            top[r, g] = m[i]
+            tot[r, g] = functools.reduce(jnp.add, p[i])
+            acc[r, g] = o[i]
 
     K = (0, 1)
     V = (2,)
     crossing = inner > 1
-    lines, cross_keys = [], []
-    for t in range(1, outer):
-        lines.append(lambda t=t: line_event(t, K))
-        if t > 1:
-            lines.append(lambda t=t: line_event(t - 1, V))
-    early = []
+    halves = [tuple(range(g, min(g + 2, key_heads))) for g in range(0, key_heads, 2)]
+    units = [functools.partial(suffix_unit, r, heads) for r in range(requests) for heads in halves]
+    early = [(5, lambda: line_event(1, K))]
     if crossing:
-        early.append((3, lambda: cross_event(1, 0, K)))
-        early.append((7, lambda: cross_event(1, 1, K)))
-    for i, event in enumerate(lines):
-        early.append((2 + i + (i > 0), event))
-    early.sort(key=lambda entry: entry[0])
+        early.append((6, lambda: cross_event(1, 0, K)))
+    early.append((8, lambda: line_event(1, V)))
+    for t in range(2, outer):
+        early.append((11 + 2 * (t - 2), lambda t=t: line_event(t, K)))
+        if crossing:
+            early.append((13 + 2 * (t - 2), lambda t=t: cross_event(1, t - 1, K)))
 
     fresh_unit()
     pl.semaphore_wait(barrier, count)
     own(K)
     own(V)
-    for r in range(requests):
-        suffix_unit(r)
-        while early and early[0][0] <= r:
+    for place, unit in enumerate(units):
+        unit()
+        while early and early[0][0] <= place:
             early.pop(0)[1]()
     for _, event in early:
         event()
     if crossing:
-        for t in range(2, outer):
-            cross_event(1, t, K)
+        cross_event(1, outer - 1, K)
 
     def far(u, kinds):
         for t in range(outer):
@@ -350,28 +377,33 @@
         return jnp.concatenate(parts, axis=0)
 
     def prior_unit(r):
-        for g in range(key_heads):
-            s = lax.dot_general(
+        heads = range(key_heads)
+        s = [
+            lax.dot_general(
                 query_rows(r, g), gathered(kbuf, r, g), NT, preferred_element_type=F32
             )
-            s = [x * factor for x in columns(s)]
-            before = top[r, g]
-            m = jnp.maximum(before, wide_max(s))
-            p = [jnp.exp2(x - m) for x in s]
-            shrink = jnp.exp2(before - m)
-            l = functools.reduce(jnp.add, p, tot[r, g] * shrink)
-            l = 1.0 / jnp.broadcast_to(jnp.sum(l, axis=1, keepdims=True), l.shape)
-            prob[r, g] = jnp.concatenate(p, axis=1).astype(BF16)
-            tot[r, g] = l
-            acc[r, g] = acc[r, g] * (shrink * l)
-
-    late = [lambda: line_event(outer - 1, V)]
+            for g in heads
+        ]
+        before = [top[r, g] for g in heads]
+        held = [tot[r, g] for g in heads]
+        s = [[x * factor for x in columns(x)] for x in s]
+        m = [jnp.maximum(b, wide_max(x)) for b, x in zip(before, s)]
+        p = [[jnp.exp2(x - most) for x in part] for part, most in zip(s, m)]
+        shrink = [jnp.exp2(b - most) for b, most in zip(before, m)]
+        l = [functools.reduce(jnp.add, part, h * k) for part, h, k in zip(p, held, shrink)]
+        l = [1.0 / jnp.broadcast_to(jnp.sum(x, axis=1, keepdims=True), x.shape) for x in l]
+        for g in heads:
+            prob[r, g] = jnp.concatenate(p[g], axis=1).astype(BF16)
+            tot[r, g] = l[g]
+            acc[r, g] = acc[r, g] * (shrink[g] * l[g])
+
+    late = [lambda t=t: line_event(t, V) for t in range(2, outer)]
     if crossing:
-        late = [lambda: cross_event(1, 0, V)] + late
+        late.insert(1, lambda: cross_event(1, 0, V))
         late += [lambda t=t: cross_event(1, t, V) for t in range(1, outer)]
     for r in range(requests):
         prior_unit(r)
-        if late and r % 2 == 0 or len(late) > 3:
+        if late:
             late.pop(0)()
     while late:
         late.pop(0)()
@@ -380,10 +412,13 @@
     whole_wait(2, 1 - core, core_recv.at[2])
 
     for r in range(requests):
+        o = [
+            jnp.dot(prob[r, g], gathered(vbuf, r, g), preferred_element_type=F32)
+            for g in range(key_heads)
+        ]
         for g in range(key_heads):
-            o = jnp.dot(prob[r, g], gathered(vbuf, r, g), preferred_element_type=F32)
-            o = (acc[r, g] + o * tot[r, g]).astype(BF16)
-            out_ref[r, :, pl.ds(g * group, group), :] = o.reshape(steps, group, width)
+            done = (acc[r, g] + o[g] * tot[r, g]).astype(BF16)
+            out_ref[r, :, pl.ds(g * group, group), :] = done.reshape(steps, group, width)
 
     for condition, copy in pending:
 
@@ -460,7 +495,7 @@
             pltpu.SemaphoreType.DMA((6,)),
             pltpu.SemaphoreType.DMA((3, half)),
             pltpu.SemaphoreType.DMA((3,)),
-            pltpu.SemaphoreType.DMA((3, 2, outer)),
+            pltpu.SemaphoreType.DMA((3, 3, outer)),
             pltpu.SemaphoreType.DMA((3, 2, half)),
             pltpu.SemaphoreType.DMA((3,)),
         ],

time: 28.3 us -> 29.2 us (1.032)
  Pallas kernels: 26.7 us -> 27.5 us
    pallas_call x1, Pallas kernels: 26.7 us -> 27.5 us  [per_device(): pl.pallas_call(kernel, out_shape=pltpu.VMEM(queries.shape, queries.dtype)...]
where the time goes in v4:
time: 29.2 us; the launch traced here: 28.9 us
  Pallas kernels  27.5 us (94%)
  local copies, waits for them, and re-layouts  0.8 us (3%)
  between operations  0.66 us (2%)
    pallas_call x1, Pallas kernels, per_device(): pl.pallas_call(kernel, out_shape=pltpu.VMEM(queries.shape, queries.dtype)...  27.5 us
    unnamed x1, local copies, waits for them, and re-layouts  0.8 us

profile of v4, /device:TPU:0, one launch (start us, length us, event | category | flops | bytes accessed | tf_op | source)
XLA Modules:
  0.0 28.9 jit_solution(17674266621376606623)
XLA Ops:
  0.7 27.5 %attend.1 = bf16[8,4,64,128]{3,2,1,0:T(8,128)(2,1)S(1)} custom-call(bf16[8,4,64,128]{3,2,1,0:T(8,128)(2,1)} %q_hbm.1, bf16[128,128]{1,0:T(8,128)(2,1)} %bitcast.11, bf16[128,128]{1,0:T(8,128)(2,1)} %bitcast.12, bf16[8,1024,128]{2,1,0:T(8,128)(2,1)} %bitcast.7, bf16[8,1024,128]{2,1,0:T(8,128)(2,1)} %bitcast.8, s32[8]{0:T(128)} %len_hbm.1, ...), custom_call_target="tpu_custom_call" | custom-call | tf_op jit(solution)/shard_map/attend/pallas_call | solution.py:467
  28.1 0.8 %copy.12 = bf16[8,4,64,128]{3,2,1,0:T(8,128)(2,1)} copy(bf16[8,4,64,128]{3,2,1,0:T(8,128)(2,1)S(1)} %attend.1) | data formatting | bytes 1048576

commit v5 on v4

--- a/solution.py
+++ b/solution.py
@@ -100,10 +100,9 @@
     for copy in loads:
         copy.start()
 
-    direct = outer <= 4
-    reach = outer if direct else 2
-    neighbours = [(pa >= d, (pa - d, pb, core)) for d in range(1, reach)]
-    neighbours += [(pa + d < outer, (pa + d, pb, core)) for d in range(1, reach)]
+    jumps = (1, 3) if outer == 4 else (1,)
+    neighbours = [(pa >= d, (pa - d, pb, core)) for d in jumps]
+    neighbours += [(pa + d < outer, (pa + d, pb, core)) for d in jumps]
     neighbours += [
         (pb > 0, (pa, pb - 1, core)),
         (pb < inner - 1, (pa, pb + 1, core)),
@@ -192,7 +191,7 @@
 
     def own(kinds):
         for kind in kinds:
-            for d in range(1, reach):
+            for d in jumps if kind != 2 else (1,):
                 for ok, a in ((pa + d < outer, pa + d), (pa >= d, pa - d)):
                     slot = jnp.clip(a, 0, outer - 1)
                     pending.append(
@@ -216,7 +215,7 @@
             a = jnp.clip(a, 0, outer - 1)
             for kind in kinds:
                 arrived(kind, a, pb, condition)
-                if not direct:
+                if kind == 2 or t + 1 < outer - 1 or len(jumps) == 1:
                     send_a(kind, a, condition, up)
                 send_b(kind, a, pb, condition, True)
                 send_b(kind, a, pb, condition, False)
@@ -320,19 +319,19 @@
     crossing = inner > 1
     halves = [tuple(range(g, min(g + 2, key_heads))) for g in range(0, key_heads, 2)]
     units = [functools.partial(suffix_unit, r, heads) for r in range(requests) for heads in halves]
-    early = [(5, lambda: line_event(1, K))]
+    early = [(1, lambda: (line_event(1, K), own(V)))]
+    for t in range(2, outer):
+        early.append((4 * t - 4 + (t > 2) * 2, lambda t=t: line_event(t, K)))
+        early.append((4 * t + (t > 2), lambda t=t: line_event(t - 1, V)))
     if crossing:
-        early.append((6, lambda: cross_event(1, 0, K)))
-    early.append((8, lambda: line_event(1, V)))
-    for t in range(2, outer):
-        early.append((11 + 2 * (t - 2), lambda t=t: line_event(t, K)))
-        if crossing:
-            early.append((13 + 2 * (t - 2), lambda t=t: cross_event(1, t - 1, K)))
+        early.append((3, lambda: cross_event(1, 0, K)))
+        for t in range(1, outer - 1):
+            early.append((3 + 4 * t, lambda t=t: cross_event(1, t, K)))
+    early.sort(key=lambda entry: entry[0])
 
     fresh_unit()
     pl.semaphore_wait(barrier, count)
     own(K)
-    own(V)
     for place, unit in enumerate(units):
         unit()
         while early and early[0][0] <= place:
@@ -397,7 +396,7 @@
             tot[r, g] = l[g]
             acc[r, g] = acc[r, g] * (shrink[g] * l[g])
 
-    late = [lambda t=t: line_event(t, V) for t in range(2, outer)]
+    late = [lambda: line_event(outer - 1, V)]
     if crossing:
         late.insert(1, lambda: cross_event(1, 0, V))
         late += [lambda t=t: cross_event(1, t, V) for t in range(1, outer)]

time: 29.2 us -> 29.9 us (1.024)
  Pallas kernels: 27.5 us -> 28.3 us
    pallas_call x1, Pallas kernels: 27.5 us -> 28.3 us  [per_device(): pl.pallas_call(kernel, out_shape=pltpu.VMEM(queries.shape, queries.dtype)...]
where the time goes in v5:
time: 29.9 us; the launch traced here: 29.8 us
  Pallas kernels  28.3 us (95%)
  local copies, waits for them, and re-layouts  0.8 us (3%)
  between operations  0.66 us (2%)
    pallas_call x1, Pallas kernels, per_device(): pl.pallas_call(kernel, out_shape=pltpu.VMEM(queries.shape, queries.dtype)...  28.3 us
    unnamed x1, local copies, waits for them, and re-layouts  0.8 us

profile of v5, /device:TPU:0, one launch (start us, length us, event | category | flops | bytes accessed | tf_op | source)
XLA Modules:
  0.0 29.8 jit_solution(5922407427908387708)
XLA Ops:
  0.7 28.3 %attend.1 = bf16[8,4,64,128]{3,2,1,0:T(8,128)(2,1)S(1)} custom-call(bf16[8,4,64,128]{3,2,1,0:T(8,128)(2,1)} %q_hbm.1, bf16[128,128]{1,0:T(8,128)(2,1)} %bitcast.11, bf16[128,128]{1,0:T(8,128)(2,1)} %bitcast.12, bf16[8,1024,128]{2,1,0:T(8,128)(2,1)} %bitcast.7, bf16[8,1024,128]{2,1,0:T(8,128)(2,1)} %bitcast.8, s32[8]{0:T(128)} %len_hbm.1, ...), custom_call_target="tpu_custom_call" | custom-call | tf_op jit(solution)/shard_map/attend/pallas_call | solution.py:466
  29.0 0.8 %copy.12 = bf16[8,4,64,128]{3,2,1,0:T(8,128)(2,1)} copy(bf16[8,4,64,128]{3,2,1,0:T(8,128)(2,1)S(1)} %attend.1) | data formatting | bytes 1048576

commit v6 on v5

--- a/solution.py
+++ b/solution.py
@@ -100,9 +100,7 @@
     for copy in loads:
         copy.start()
 
-    jumps = (1, 3) if outer == 4 else (1,)
-    neighbours = [(pa >= d, (pa - d, pb, core)) for d in jumps]
-    neighbours += [(pa + d < outer, (pa + d, pb, core)) for d in jumps]
+    neighbours = [(pa >= 1, (pa - 1, pb, core)), (pa + 1 < outer, (pa + 1, pb, core))]
     neighbours += [
         (pb > 0, (pa, pb - 1, core)),
         (pb < inner - 1, (pa, pb + 1, core)),
@@ -191,7 +189,7 @@
 
     def own(kinds):
         for kind in kinds:
-            for d in jumps if kind != 2 else (1,):
+            for d in (1,):
                 for ok, a in ((pa + d < outer, pa + d), (pa >= d, pa - d)):
                     slot = jnp.clip(a, 0, outer - 1)
                     pending.append(
@@ -215,8 +213,7 @@
             a = jnp.clip(a, 0, outer - 1)
             for kind in kinds:
                 arrived(kind, a, pb, condition)
-                if kind == 2 or t + 1 < outer - 1 or len(jumps) == 1:
-                    send_a(kind, a, condition, up)
+                send_a(kind, a, condition, up)
                 send_b(kind, a, pb, condition, True)
                 send_b(kind, a, pb, condition, False)
                 send_core(kind, a, pb, condition)
@@ -319,19 +316,19 @@
     crossing = inner > 1
     halves = [tuple(range(g, min(g + 2, key_heads))) for g in range(0, key_heads, 2)]
     units = [functools.partial(suffix_unit, r, heads) for r in range(requests) for heads in halves]
-    early = [(1, lambda: (line_event(1, K), own(V)))]
-    for t in range(2, outer):
-        early.append((4 * t - 4 + (t > 2) * 2, lambda t=t: line_event(t, K)))
-        early.append((4 * t + (t > 2), lambda t=t: line_event(t - 1, V)))
+    early = []
+    for t in range(1, outer):
+        early.append((5 * t - 1 - (t > 2), lambda t=t: line_event(t, K)))
+        early.append((4 * t + 3, lambda t=t: line_event(t, V)))
     if crossing:
-        early.append((3, lambda: cross_event(1, 0, K)))
-        for t in range(1, outer - 1):
-            early.append((3 + 4 * t, lambda t=t: cross_event(1, t, K)))
+        early.append((5, lambda: cross_event(1, 0, K)))
+        early.append((12, lambda: cross_event(1, 1, K)))
     early.sort(key=lambda entry: entry[0])
 
     fresh_unit()
     pl.semaphore_wait(barrier, count)
     own(K)
+    own(V)
     for place, unit in enumerate(units):
         unit()
         while early and early[0][0] <= place:
@@ -339,7 +336,8 @@
     for _, event in early:
         event()
     if crossing:
-        cross_event(1, outer - 1, K)
+        for t in range(2, outer):
+            cross_event(1, t, K)
 
     def far(u, kinds):
         for t in range(outer):
@@ -396,9 +394,9 @@
             tot[r, g] = l[g]
             acc[r, g] = acc[r, g] * (shrink[g] * l[g])
 
-    late = [lambda: line_event(outer - 1, V)]
+    late = []
     if crossing:
-        late.insert(1, lambda: cross_event(1, 0, V))
+        late = [lambda: cross_event(1, 0, V)]
         late += [lambda t=t: cross_event(1, t, V) for t in range(1, outer)]
     for r in range(requests):
         prior_unit(r)

time: 29.9 us -> 27.4 us (0.916)
  Pallas kernels: 28.3 us -> 25.8 us
    pallas_call x1, Pallas kernels: 28.3 us -> 25.8 us  [per_device(): pl.pallas_call(kernel, out_shape=pltpu.VMEM(queries.shape, queries.dtype)...]
where the time goes in v6:
time: 27.4 us; the launch traced here: 27.2 us
  Pallas kernels  25.8 us (94%)
  local copies, waits for them, and re-layouts  0.8 us (3%)
  between operations  0.66 us (2%)
    pallas_call x1, Pallas kernels, per_device(): pl.pallas_call(kernel, out_shape=pltpu.VMEM(queries.shape, queries.dtype)...  25.8 us
    unnamed x1, local copies, waits for them, and re-layouts  0.8 us

profile of v6, /device:TPU:0, one launch (start us, length us, event | category | flops | bytes accessed | tf_op | source)
XLA Modules:
  0.0 27.2 jit_solution(2649455108820696757)
XLA Ops:
  0.7 25.8 %attend.1 = bf16[8,4,64,128]{3,2,1,0:T(8,128)(2,1)S(1)} custom-call(bf16[8,4,64,128]{3,2,1,0:T(8,128)(2,1)} %q_hbm.1, bf16[128,128]{1,0:T(8,128)(2,1)} %bitcast.11, bf16[128,128]{1,0:T(8,128)(2,1)} %bitcast.12, bf16[8,1024,128]{2,1,0:T(8,128)(2,1)} %bitcast.7, bf16[8,1024,128]{2,1,0:T(8,128)(2,1)} %bitcast.8, s32[8]{0:T(128)} %len_hbm.1, ...), custom_call_target="tpu_custom_call" | custom-call | tf_op jit(solution)/shard_map/attend/pallas_call | solution.py:464
  26.4 0.8 %copy.12 = bf16[8,4,64,128]{3,2,1,0:T(8,128)(2,1)} copy(bf16[8,4,64,128]{3,2,1,0:T(8,128)(2,1)S(1)} %attend.1) | data formatting | bytes 1048576

commit v7 on v6

--- a/solution.py
+++ b/solution.py
@@ -318,8 +318,8 @@
     units = [functools.partial(suffix_unit, r, heads) for r in range(requests) for heads in halves]
     early = []
     for t in range(1, outer):
-        early.append((5 * t - 1 - (t > 2), lambda t=t: line_event(t, K)))
-        early.append((4 * t + 3, lambda t=t: line_event(t, V)))
+        early.append((4 * t - (t > 2), lambda t=t: line_event(t, K)))
+        early.append((4 * t + 2 - (t > 2), lambda t=t: line_event(t, V)))
     if crossing:
         early.append((5, lambda: cross_event(1, 0, K)))
         early.append((12, lambda: cross_event(1, 1, K)))

time: 27.4 us -> 27.4 us (level)
  no operation moved by 1% of the time
where the time goes in v7:
time: 27.4 us; the launch traced here: 27.2 us
  Pallas kernels  25.8 us (94%)
  local copies, waits for them, and re-layouts  0.8 us (3%)
  between operations  0.66 us (2%)
    pallas_call x1, Pallas kernels, per_device(): pl.pallas_call(kernel, out_shape=pltpu.VMEM(queries.shape, queries.dtype)...  25.8 us
    unnamed x1, local copies, waits for them, and re-layouts  0.8 us

profile of v7, /device:TPU:0, one launch (start us, length us, event | category | flops | bytes accessed | tf_op | source)
XLA Modules:
  0.0 27.2 jit_solution(1206758124524412462)
XLA Ops:
  0.7 25.8 %attend.1 = bf16[8,4,64,128]{3,2,1,0:T(8,128)(2,1)S(1)} custom-call(bf16[8,4,64,128]{3,2,1,0:T(8,128)(2,1)} %q_hbm.1, bf16[128,128]{1,0:T(8,128)(2,1)} %bitcast.11, bf16[128,128]{1,0:T(8,128)(2,1)} %bitcast.12, bf16[8,1024,128]{2,1,0:T(8,128)(2,1)} %bitcast.7, bf16[8,1024,128]{2,1,0:T(8,128)(2,1)} %bitcast.8, s32[8]{0:T(128)} %len_hbm.1, ...), custom_call_target="tpu_custom_call" | custom-call | tf_op jit(solution)/shard_map/attend/pallas_call | solution.py:464
  26.4 0.8 %copy.12 = bf16[8,4,64,128]{3,2,1,0:T(8,128)(2,1)} copy(bf16[8,4,64,128]{3,2,1,0:T(8,128)(2,1)S(1)} %attend.1) | data formatting | bytes 1048576
